TPU v7x, 256 devices: a whole 4x4x8 slice. The times are simulated.
256 devices in a mesh: lat: 16 (over x, y), lev: 16 (over z, core).
Axes of the slice: x: 4, y: 4, z: 8, core: 2. Of those that a mesh axis runs over, the one named last changes fastest.
Arguments:
- grid: bfloat16 [64, 1280, 2560], P('lev', 'lat'), may hold values from -6 to 6
- pair_index: int32 [512], replicated, may hold values from 1 to 639, as said below
- legendre: bfloat16 [512, 1280, 1280], P('lev', 'lat'), may hold values from -0.15625 to 0.15625
- vertical: bfloat16 [64, 64], replicated, may hold values from -0.75 to 0.75
Outputs:
- spectral: bfloat16 [16, 32, 1280, 128], P('lev', 'lat')
Inputs may be any that keep to these rules, and one draw needn't show every extreme that they name: `pair_index`: distinct pair numbers; pair p holds wavenumbers p and 1280 - p.
All inputs are finite; a program needn't handle non-finite values.
Results may differ from a plain program's by a relative error of at most 0.017.
Values may be sent and summed in bfloat16 or wider, within the bound.
A program may use at most 192 MiB of HBM per device.

v0:
```python
import math

import jax
import jax.numpy as jnp
from jax import lax
from jax.sharding import PartitionSpec as P

NDEG = 1280


def fourier_table(pair_index, nlon):
    pairs = pair_index.shape[0]
    wavenumbers = jnp.stack([pair_index, NDEG - pair_index], axis=1)
    longitude = jnp.arange(nlon, dtype=jnp.int32)
    phase = longitude[:, None, None] * wavenumbers[None, :, :] % nlon
    angle = phase.astype(jnp.float32) * jnp.float32(2.0 * math.pi / nlon)
    factor = jnp.float32(1.0 / math.sqrt(nlon))
    table = jnp.stack([jnp.cos(angle) * factor, -jnp.sin(angle) * factor], axis=-1)
    return table.reshape(nlon, pairs * 4).astype(jnp.bfloat16)


def legendre_block(rows_table, slot_four, pairs_here):
    slots, _, spec_rows = rows_table.shape
    levels = slot_four.shape[0]
    both = jnp.einsum("skr,lksuc->surcl", rows_table, slot_four, preferred_element_type=jnp.float32)
    both = both.reshape(slots, 2, spec_rows, 2 * levels)
    row_ids = jnp.arange(spec_rows, dtype=jnp.int32)
    first = row_ids[None, :] < (NDEG - pairs_here)[:, None]
    return jnp.where(first[:, :, None], both[:, 0], both[:, 1])


def body(grid, pair_index, legendre, vertical):
    lev_dev, lat_dev, nlon = grid.shape
    pairs = pair_index.shape[0]
    n_lev = lax.axis_size("lev")
    n_lat = lax.axis_size("lat")
    lev_slots = pairs // n_lev
    pair_dev = lev_slots // n_lat
    table = fourier_table(pair_index, nlon)
    fourier = jnp.dot(
        grid.reshape(lev_dev * lat_dev, nlon), table, preferred_element_type=jnp.float32
    )
    fourier = fourier.astype(jnp.bfloat16).reshape(lev_dev, lat_dev, pairs * 4)
    fourier = lax.all_to_all(fourier, "lev", split_axis=2, concat_axis=0, tiled=True)
    levels = fourier.shape[0]
    pairs_lev = lax.dynamic_slice_in_dim(
        pair_index, lax.axis_index("lev") * lev_slots, lev_slots, 0
    )
    pairs_own = lax.dynamic_slice_in_dim(pairs_lev, lax.axis_index("lat") * pair_dev, pair_dev, 0)
    gathered = lax.all_to_all(fourier, "lat", split_axis=2, concat_axis=1, tiled=True)
    whole_table = lax.all_to_all(legendre, "lat", split_axis=0, concat_axis=1, tiled=True)
    slot_four = gathered.reshape(levels, gathered.shape[1], pair_dev, 2, 2)
    coef = legendre_block(whole_table, slot_four, pairs_own)
    coef = coef.astype(jnp.bfloat16)
    spec_rows = coef.shape[1]
    coef = coef.reshape(pair_dev, spec_rows, 2, levels)
    mixed = jnp.einsum("srcl,ml->srcm", coef, vertical, preferred_element_type=jnp.float32)
    return mixed.astype(jnp.bfloat16).reshape(1, pair_dev, spec_rows, 2 * levels)


def solution(mesh):
    placed = (P("lev", "lat", None), P(), P("lev", "lat", None), P())
    return jax.shard_map(
        body, mesh=mesh, in_specs=placed, out_specs=P("lev", "lat", None, None), check_vma=False
    )
```

profile of v0, /device:TPU:28, one launch (start us, length us, event | category | flops | bytes accessed | tf_op | source)
XLA Modules:
  0.0 345.8 jit_solution(15760677969006155593)
XLA Ops:
  0.0 0.8 broadcast_subtract_fusion
  0.8 0.7 pad_add_fusion
  1.5 45.8 %multiply_convert_fusion.1 = (bf16[2560,512,2,1]{1,0,3,2:T(8,128)(2,1)}, bf16[2560,512,2,1]{1,0,3,2:T(8,128)(2,1)}) fusion(s32[512,2]{0,1:T(2,128)S(1)} %pad_add_fusion), kind=kLoop, calls=%fused_computation.5 | loop fusion | flops 36700160 | bytes 10489856 | tf_op jit(solution)/shard_map/convert
  47.2 9.0 %pad_maximum_fusion = bf16[2560,512,2,2]{1,0,3,2:T(8,128)(2,1)} fusion(bf16[2560,512,2,1]{1,0,3,2:T(8,128)(2,1)} %get-tuple-element.8, bf16[2560,512,2,1]{1,0,3,2:T(8,128)(2,1)} %get-tuple-element.7), kind=kLoop, calls=%fused_computation.3 | loop fusion | flops 5242880 | bytes 20971520 | tf_op jit(solution)/shard_map/stack | solution.py:18
  56.2 26.6 %copy.27 = bf16[2560,512,2,2]{0,3,2,1:T(2,128)(2,1)} copy(bf16[2560,512,2,2]{1,0,3,2:T(8,128)(2,1)} %pad_maximum_fusion) | data formatting | bytes 20971520 | tf_op jit(solution)/shard_map/stack | solution.py:18
  82.8 21.9 %convert_element_type.38 = bf16[2560,2048]{0,1:T(8,128)(2,1)} reshape(bf16[2560,512,2,2]{0,3,2,1:T(2,128)(2,1)} %copy.27) | data formatting | bytes 20971520 | tf_op jit(solution)/shard_map/convert_element_type | solution.py:19
  104.7 7.5 %convolution_convert_fusion = bf16[2048,320]{0,1:T(8,128)(2,1)S(1)} fusion(bf16[2560,2048]{0,1:T(8,128)(2,1)} %convert_element_type.38, bf16[320,2560]{1,0:T(8,128)(2,1)S(1)} %bitcast.43), kind=kOutput, calls=%fused_computation.10 | convolution fusion | flops 3356098560 | bytes 13434880 | tf_op jit(solution)/shard_map/dot_general | solution.py:40
  112.3 2.5 copy.28
  114.8 58.4 %all_to_all.51 = bf16[4,80,2048]{1,0,2:T(4,128)(2,1)} all-to-all(bf16[4,80,2048]{1,0,2:T(4,128)(2,1)} %copy.28), channel_id=1, replica_groups=mesh['lat'=16,'lev'=16] {'lev'}, dimensions={2} | all-to-all | bytes 2621440 | tf_op jit(solution)/shard_map/all_to_all | solution.py:44
  173.2 2.8 copy.39
  176.1 3.2 copy.31
  179.3 32.7 %all_to_all.52 = bf16[64,80,128]{1,0,2:T(8,128)(2,1)} all-to-all(bf16[64,80,128]{1,0,2:T(8,128)(2,1)} %copy.31), channel_id=1, replica_groups=mesh['lat'=16,'lev'=16] {'lat'}, dimensions={2} | all-to-all | bytes 2621440 | tf_op jit(solution)/shard_map/all_to_all | solution.py:50
  212.0 8.0 %all-to-all-start.2 = ((bf16[32,80,1280]{2,1,0:T(8,128)(2,1)}), bf16[32,80,1280]{2,1,0:T(8,128)(2,1)}, u32[]{:S(2)}, u32[]{:S(2)}) async-start(bf16[32,80,1280]{2,1,0:T(8,128)(2,1)} %param.6), calls=%async_computation.2 | async-start | bytes 13107200 | tf_op jit(solution)/shard_map/all_to_all | solution.py:51
  220.1 0.8 dynamic-slice_subtract_fusion
  220.8 0.1 iota_compare_fusion
  220.9 4.3 %copy.33 = bf16[64,16,80,8]{2,1,0,3:T(8,128)(2,1)} copy(bf16[64,16,80,8]{2,0,3,1:T(8,128)(2,1)} %bitcast.44) | data formatting | bytes 2621440 | tf_op jit(solution)/shard_map/all_to_all | solution.py:50
  225.3 3.7 %reshape.96 = bf16[64,1280,2,2,2]{1,0,4,3,2:T(8,128)(2,1)S(1)} reshape(bf16[64,16,80,8]{2,1,0,3:T(8,128)(2,1)} %copy.33) | data formatting | bytes 2621440 | tf_op jit(solution)/shard_map/reshape | solution.py:52
  229.0 110.1 %all-to-all-done.2 = bf16[32,80,1280]{2,1,0:T(8,128)(2,1)} async-done(((bf16[32,80,1280]{2,1,0:T(8,128)(2,1)}), bf16[32,80,1280]{2,1,0:T(8,128)(2,1)}, u32[]{:S(2)}, u32[]{:S(2)}) %all-to-all-start.2) | async-done | bytes 6553632 | tf_op jit(solution)/shard_map/all_to_all | solution.py:51
  339.1 3.3 copy.34
  342.4 0.0 copy-start.2
  342.4 1.9 fusion.8
  344.3 0.1 fusion.7
  344.4 0.3 convolution_convert_fusion.1
  344.7 1.1 copy.35
  (5 shorter events, 0.0 us)
Async XLA Ops:
  0.0 104.7 %copy-start = (bf16[4,80,2560]{2,1,0:T(8,128)(2,1)S(1)}, bf16[4,80,2560]{2,1,0:T(8,128)(2,1)}, u32[]{:S(2)}) copy-start(bf16[4,80,2560]{2,1,0:T(8,128)(2,1)} %param.4) | copy-start | bytes 4915204
  212.0 127.0 %all-to-all-start.2 = ((bf16[32,80,1280]{2,1,0:T(8,128)(2,1)}), bf16[32,80,1280]{2,1,0:T(8,128)(2,1)}, u32[]{:S(2)}, u32[]{:S(2)}) async-start(bf16[32,80,1280]{2,1,0:T(8,128)(2,1)} %param.6), calls=%async_computation.2 | async-start | bytes 13107200 | tf_op jit(solution)/shard_map/all_to_all | solution.py:51
  342.4 2.0 copy-start.2
  342.4 3.4 copy-start.1
where the time goes:
time: 347 us; the launch traced here: 346 us
  waiting for transfers between devices  110 us (32%)
  blocking collectives  91.2 us (26%)
  local copies, waits for them, and re-layouts  69.6 us (20%)
  other arithmetic  57.1 us (16%)
  matrix products  9.76 us (3%)
  starting transfers between devices  8.04 us (2%)
    all_to_all x1, waiting for transfers between devices, body(): lax.all_to_all(legendre, 'lat', split_axis=0, concat_axis=1, tiled=True)  110 us
    all_to_all x1, blocking collectives, body(): lax.all_to_all(fourier, 'lev', split_axis=2, concat_axis=0, tiled=True)  58.4 us
    another operation x1, other arithmetic  45.8 us
    all_to_all x1, blocking collectives, body(): lax.all_to_all(fourier, 'lat', split_axis=2, concat_axis=1, tiled=True)  32.7 us
    another operation x1, local copies, waits for them, and re-layouts, fourier_table(): jnp.stack([jnp.cos(angle) * factor, -jnp.sin(angle) * factor], axis=-1)  26.6 us
    convert_element_type x1, local copies, waits for them, and re-layouts, fourier_table(): return table.reshape(nlon, pairs * 4).astype(jnp.bfloat16)  21.9 us
    another operation x1, other arithmetic, fourier_table(): jnp.stack([jnp.cos(angle) * factor, -jnp.sin(angle) * factor], axis=-1)  8.98 us
    all_to_all x1, starting transfers between devices, body(): lax.all_to_all(legendre, 'lat', split_axis=0, concat_axis=1, tiled=True)  8.04 us
  transfers between devices with their start and end apart: 1, of which 1 were waited for; matrix products, arithmetic and copies ran while one was open for 3% of the time, Pallas kernels for 0%

commit v1 on v0

v1 whole, which is shorter than its diff:
```python
import functools
import math

import jax
import jax.numpy as jnp
from jax import lax
from jax.sharding import PartitionSpec as P
from jax.experimental import pallas as pl
from jax.experimental.pallas import tpu as pltpu

MESH = pl.DeviceIdType.MESH
F32 = jnp.float32
BF16 = jnp.bfloat16
NLON = 2560
NDEG = 1280
ROWS = 1280
LOW = 64
HIGH = NLON // LOW
DIST = (2, 1, 3, 0)


def iota(shape, dim):
    return lax.broadcasted_iota(jnp.int32, shape, dim)


def cos_sin(turns_num):
    whole = jnp.floor(turns_num * F32(1.0 / NLON) + F32(0.5))
    h = (turns_num - whole * F32(NLON)) * F32(math.pi / NLON)
    h2 = h * h
    s = F32(-1.0 / 39916800.0)
    for c in (1.0 / 362880.0, -1.0 / 5040.0, 1.0 / 120.0, -1.0 / 6.0, 1.0):
        s = s * h2 + F32(c)
    s = s * h
    c_ = F32(1.0 / 479001600.0)
    for c in (-1.0 / 3628800.0, 1.0 / 40320.0, -1.0 / 720.0, 1.0 / 24.0, -0.5, 1.0):
        c_ = c_ * h2 + F32(c)
    return F32(1.0) - F32(2.0) * s * s, F32(2.0) * s * c_


def kernel(pair_ref, leg, grid_hbm, pcol, vert, out,
           grid, gsign, table, base_a, base_b, base_c, base_s, xs, xr, perm, zs, zr,
           wide, mixed, leg1, leg2, rs, rr,
           grid_sem, legl_sem, legs_sem, legr_sem, xs_sem, xr_sem, zl_sem, zs_sem, zr_sem, rs_sem, rr_sem):
    lat = lax.axis_index("lat")
    lev = lax.axis_index("lev")
    x, y = lat // 4, lat % 4

    def at_x(d):
        return (lax.rem(x + d, 4) * 4 + y, lev)

    def at_y(d):
        return (x * 4 + lax.rem(y + d, 4), lev)

    def at_z(e):
        return (lat, lax.rem(lev + e, 16))

    barrier = pltpu.get_barrier_semaphore()
    peers = [at_x(d) for d in (1, 2, 3)] + [at_y(d) for d in (1, 2, 3)] + [at_z(e) for e in range(1, 16)]
    for peer in peers:
        pl.semaphore_signal(barrier, inc=1, device_id=peer, device_id_type=MESH)

    grid_copy = pltpu.make_async_copy(grid_hbm, grid, grid_sem)
    grid_copy.start()

    local = []
    for n, d in enumerate(DIST):
        sy, sx = lax.rem(y + d, 4), lax.rem(x + d, 4)
        local.append((
            pltpu.make_async_copy(leg.at[x, sy, 0], leg1.at[sy, pl.ds(x * 5, 5)], legl_sem.at[0, d]),
            pltpu.make_async_copy(leg.at[sx, y, 1], leg2.at[sx, pl.ds(4 + y * 5, 5)], legl_sem.at[1, d]),
        ))
    for pair in local:
        for copy in pair:
            copy.start()
    leg1[:, 20:24] = jnp.zeros((4, 4, 16, ROWS), BF16)
    leg2[:, 0:4] = jnp.zeros((4, 4, 16, ROWS), BF16)

    remote = []
    for d in DIST:
        sy, sx = lax.rem(y + d, 4), lax.rem(x + d, 4)
        group = []
        for e in (2, 1, 3):
            px, py = lax.rem(x + e, 4), lax.rem(y + e, 4)
            group.append(pltpu.make_async_remote_copy(
                src_ref=leg.at[px, sy, 0], dst_ref=leg1.at[sy, pl.ds(x * 5, 5)],
                send_sem=legs_sem.at[0, d, e], recv_sem=legr_sem.at[0, d, e],
                device_id=at_x(e), device_id_type=MESH))
            group.append(pltpu.make_async_remote_copy(
                src_ref=leg.at[sx, py, 1], dst_ref=leg2.at[sx, pl.ds(4 + y * 5, 5)],
                send_sem=legs_sem.at[1, d, e], recv_sem=legr_sem.at[1, d, e],
                device_id=at_y(e), device_id_type=MESH))
        remote.append(group)

    row, col = iota((256, 256), 0), iota((256, 256), 1)
    want = ((row // 8) % 2) * 128 + (row // 16) * 8 + row % 8
    sign = jnp.where(((row // 8) % 2 == 1) & (row % 2 == 1), F32(-1.0), F32(1.0))
    perm[...] = jnp.where(col == want, sign, F32(0.0)).astype(BF16)

    def make_base(d, h):
        dest = lax.rem((x if h == 0 else y) + d, 4)
        p = pcol[h, dest]
        low = iota((LOW, 128), 0).astype(F32)
        cos, sin = cos_sin(low * p)
        base_c[...] = cos
        base_s[...] = sin
        high = (iota((HIGH, 128), 0) * LOW).astype(F32)
        cos, sin = cos_sin(high * p)
        imag = iota((HIGH, 128), 1) % 2 == 1
        factor = F32(1.0 / math.sqrt(NLON))
        base_a[...] = jnp.where(imag, -sin, cos) * factor
        base_b[...] = jnp.where(imag, -cos, -sin) * factor

    def make_table(d):
        for h in range(2):
            make_base(d, h)

            @pl.loop(0, HIGH // 8)
            def _(g):
                a = base_a[pl.ds(pl.multiple_of(g * 8, 8), 8)]
                b = base_b[pl.ds(pl.multiple_of(g * 8, 8), 8)]
                for i in range(8):
                    block = a[i:i + 1] * base_c[...] + b[i:i + 1] * base_s[...]
                    first = pl.multiple_of((g * 8 + i) * LOW, LOW)
                    table[pl.ds(first, LOW), h * 128:(h + 1) * 128] = block.astype(BF16)

    make_table(DIST[0])
    grid_copy.wait()
    odd = iota((320, NLON), 1) % 2 == 1
    flat = grid[...].reshape(320, NLON)
    gsign[...] = jnp.where(odd, -flat, flat)

    pl.semaphore_wait(barrier, len(peers))
    for copy in remote[0]:
        copy.start()

    x_copies = []
    for n, d in enumerate(DIST):
        if n > 0:
            make_table(d)
        for u in range(2):
            source = grid[...].reshape(320, NLON) if u == 0 else gsign[...]
            four = jnp.dot(source, table[...], preferred_element_type=F32).astype(BF16)
            for h in range(2):
                part = four[:, h * 128:(h + 1) * 128].reshape(4, 80, 128)
                if d == 0:
                    own = x if h == 0 else 4 + y
                    xr[:, own, :, u * 128:(u + 1) * 128] = part
                else:
                    xs[d - 1, h, :, :, u * 128:(u + 1) * 128] = part
        if d > 0:
            for h in range(2):
                copy = pltpu.make_async_remote_copy(
                    src_ref=xs.at[d - 1, h], dst_ref=xr.at[:, x if h == 0 else 4 + y],
                    send_sem=xs_sem.at[h, d], recv_sem=xr_sem.at[h, d],
                    device_id=at_x(d) if h == 0 else at_y(d), device_id_type=MESH)
                copy.start()
                x_copies.append(copy)
    for copy in remote[1]:
        copy.start()

    level_of = (iota((64, 1024), 1) // 16 == iota((64, 1024), 0)).astype(BF16)
    spread = jnp.dot(vert[...], level_of, preferred_element_type=F32)
    inner = iota((64, 1024), 1) % 16
    for s in range(4):
        for u in range(2):
            for c in range(2):
                i = s * 4 + u * 2 + c
                wide[i * 64:(i + 1) * 64, :] = jnp.where(inner == u * 8 + s * 2 + c, spread, F32(0.0)).astype(BF16)

    for copy in x_copies:
        copy.wait()
    for l in range(4):
        turned = lax.dot_general(perm[...], xr[l].reshape(640, 256), (((1,), (1,)), ((), ())),
                                 preferred_element_type=F32).astype(BF16)
        zs[:, l] = turned.reshape(16, 16, 640)
    z_copies = []
    for e in (8, 7, 9, 6, 10, 5, 11, 4, 12, 3, 13, 2, 14, 1, 15):
        copy = pltpu.make_async_remote_copy(
            src_ref=zs.at[lax.rem(lev + e, 16)], dst_ref=zr.at[lev],
            send_sem=zs_sem.at[e], recv_sem=zr_sem.at[e],
            device_id=at_z(e), device_id_type=MESH)
        copy.start()
        z_copies.append(copy)
    z_own = pltpu.make_async_copy(zs.at[lev], zr.at[lev], zl_sem)
    z_own.start()
    for group in remote[2:]:
        for copy in group:
            copy.start()
    z_own.wait()
    for copy in z_copies:
        copy.wait()
    mixed[...] = jnp.dot(wide[...], zr[...].reshape(1024, 640), preferred_element_type=F32).astype(BF16)

    out_copies = []
    for n, d in enumerate(DIST):
        for copy in local[n]:
            copy.wait()
        for copy in remote[n]:
            copy.wait()
        for h in range(2):
            s = lax.rem((y if h == 0 else x) + d, 4)
            slot = lev * 32 + (x * 4 + s) * 2 if h == 0 else lev * 32 + (s * 4 + y) * 2 + 1
            p = pair_ref[slot]
            legs = leg1 if h == 0 else leg2
            lanes = slice(0, 384) if h == 0 else slice(256, 640)
            g = mixed[pl.ds(pl.multiple_of(s * 256, 256), 256), lanes]
            half = ROWS // 2
            left = jnp.dot(g[0:128], legs[s, :, :, 0:half].reshape(384, half), preferred_element_type=F32)
            both = jnp.dot(g, legs[s, :, :, half:ROWS].reshape(384, half), preferred_element_type=F32)
            first = iota((128, half), 1) + half < NDEG - p
            right = jnp.where(first, both[0:128], both[128:256])
            dest = rr.at[h, 0] if d == 0 else rs.at[h, d - 1]
            dest[:, 0:half] = left.astype(BF16)
            dest[:, half:ROWS] = right.astype(BF16)
            if d > 0:
                copy = pltpu.make_async_remote_copy(
                    src_ref=rs.at[h, d - 1], dst_ref=rr.at[h, d],
                    send_sem=rs_sem.at[h, d], recv_sem=rr_sem.at[h, d],
                    device_id=at_y(d) if h == 0 else at_x(d), device_id_type=MESH)
                copy.start()
                out_copies.append(copy)
    for copy in out_copies:
        copy.wait()
    for h in range(2):
        for r in range(0, ROWS, 256):
            total = rr[h, 0, :, r:r + 256].astype(F32)
            for d in (1, 2, 3):
                total = total + rr[h, d, :, r:r + 256].astype(F32)
            out[0, h, r:r + 256, :] = total.T.astype(BF16)


def body(grid, pair_index, legendre, vertical):
    slots = pair_index.reshape(16, 4, 4, 2)
    over_x = slots[:, :, :, 0].transpose(1, 0, 2).reshape(4, 64)
    over_y = slots[:, :, :, 1].transpose(2, 0, 1).reshape(4, 64)
    pcol = jnp.repeat(jnp.stack([over_x, over_y]), 2, axis=-1).astype(F32).reshape(2, 4, 1, 128)
    vmem = pl.BlockSpec(memory_space=pltpu.VMEM)
    hbm = pl.BlockSpec(memory_space=pl.ANY)
    dma = pltpu.SemaphoreType.DMA
    return pl.pallas_call(
        kernel,
        out_shape=jax.ShapeDtypeStruct((1, 2, ROWS, 128), BF16),
        in_specs=[pl.BlockSpec(memory_space=pltpu.SMEM), hbm, hbm, vmem, vmem],
        out_specs=vmem,
        scratch_shapes=[
            pltpu.VMEM((4, 80, NLON), BF16),
            pltpu.VMEM((320, NLON), BF16),
            pltpu.VMEM((NLON, 256), BF16),
            pltpu.VMEM((HIGH, 128), F32),
            pltpu.VMEM((HIGH, 128), F32),
            pltpu.VMEM((LOW, 128), F32),
            pltpu.VMEM((LOW, 128), F32),
            pltpu.VMEM((3, 2, 4, 80, 256), BF16),
            pltpu.VMEM((4, 8, 80, 256), BF16),
            pltpu.VMEM((256, 256), BF16),
            pltpu.VMEM((16, 4, 16, 640), BF16),
            pltpu.VMEM((16, 4, 16, 640), BF16),
            pltpu.VMEM((1024, 1024), BF16),
            pltpu.VMEM((1024, 640), BF16),
            pltpu.VMEM((4, 24, 16, ROWS), BF16),
            pltpu.VMEM((4, 24, 16, ROWS), BF16),
            pltpu.VMEM((2, 3, 128, ROWS), BF16),
            pltpu.VMEM((2, 4, 128, ROWS), BF16),
            dma, dma((2, 4)), dma((2, 4, 4)), dma((2, 4, 4)), dma((2, 4)), dma((2, 4)),
            dma, dma((16,)), dma((16,)), dma((2, 4)), dma((2, 4)),
        ],
        compiler_params=pltpu.CompilerParams(
            collective_id=0, has_side_effects=True, vmem_limit_bytes=56 * 1024 * 1024),
        cost_estimate=pl.CostEstimate(flops=8_000_000_000, bytes_accessed=12_000_000, transcendentals=0),
        name="spectral",
    )(pair_index, legendre.reshape(4, 4, 2, 5, 16, ROWS), grid, pcol, vertical)


def solution(mesh):
    placed = (P("lev", "lat", None), P(), P("lev", "lat", None), P())
    return jax.shard_map(
        body, mesh=mesh, in_specs=placed, out_specs=P("lev", "lat", None, None), check_vma=False
    )
```

time: 347 us -> 88.7 us (0.26)
  the two profiles are of different devices: /device:TPU:28 before, /device:TPU:1 now
where the time goes in v1:
time: 88.7 us; the launch traced here: 88.5 us
  Pallas kernels  83.9 us (95%)
  local copies, waits for them, and re-layouts  4.55 us (5%)
    pallas_call x1, Pallas kernels, body(): pl.pallas_call(kernel, out_shape=jax.ShapeDtypeStruct((1, 2, ROWS, 128),...  83.9 us
    unnamed x1, local copies, waits for them, and re-layouts  1.97 us

profile of v1, /device:TPU:1, one launch (start us, length us, event | category | flops | bytes accessed | tf_op | source)
XLA Modules:
  0.0 88.5 jit_solution(1325975090428680835)
XLA Ops:
  0.0 0.9 reshape.20
  0.9 0.1 fusion
  1.0 0.2 copy.10
  1.2 0.2 copy.12
  1.4 0.1 copy.13
  1.5 0.1 stack_reshape.7
  1.6 0.1 copy.11
  1.7 0.1 stack_reshape.6
  1.8 0.1 copy.14
  2.0 0.7 copy.15.pcol
  2.6 83.9 %spectral.1 = bf16[1,2,1280,128]{3,2,1,0:T(8,128)(2,1)} custom-call(s32[512]{0:T(512)} %pair_ref.1, bf16[4,4,2,5,16,1280]{5,4,3,2,1,0:T(8,128)(2,1)} %bitcast.11, bf16[4,80,2560]{2,1,0:T(8,128)(2,1)} %grid_hbm.1, f32[2,4,1,128]{3,2,1,0:T(1,128)} %copy.15.pcol, bf16[64,64]{1,0:T(8,128)(2,1)} %vert.1), custom_call_target="tpu_custom_call" | custom-call | flops 8000000000 | bytes 12000000 | tf_op jit(solution)/shard_map/spectral/pallas_call | solution.py:240
  86.5 2.0 %copy.17 = bf16[1,2,1280,128]{3,2,1,0:T(8,128)(2,1)} copy(bf16[1,2,1280,128]{3,2,1,0:T(8,128)(2,1)} %spectral.1) | data formatting | bytes 1310720
  (2 shorter events, 0.1 us)

commit v2 on v0

v2 whole, which is shorter than its diff:
```python
import math

import jax
import jax.numpy as jnp
from jax import lax
from jax.sharding import PartitionSpec as P
from jax.experimental import pallas as pl
from jax.experimental.pallas import tpu as pltpu

MESH = pl.DeviceIdType.MESH
F32 = jnp.float32
BF16 = jnp.bfloat16
NLON = 2560
NDEG = 1280
ROWS = 1280
HALF = ROWS // 2
LOW = 64
HIGH = NLON // 2 // LOW
DIST = (2, 1, 3, 0)


def iota(shape, dim):
    return lax.broadcasted_iota(jnp.int32, shape, dim)


def cos_sin(number):
    whole = jnp.floor(number * F32(1.0 / NLON) + F32(0.5))
    h = (number - whole * F32(NLON)) * F32(math.pi / NLON)
    h2 = h * h
    s = F32(-1.0 / 39916800.0)
    for c in (1.0 / 362880.0, -1.0 / 5040.0, 1.0 / 120.0, -1.0 / 6.0, 1.0):
        s = s * h2 + F32(c)
    s = s * h
    c_ = F32(1.0 / 479001600.0)
    for c in (-1.0 / 3628800.0, 1.0 / 40320.0, -1.0 / 720.0, 1.0 / 24.0, -0.5, 1.0):
        c_ = c_ * h2 + F32(c)
    return F32(1.0) - F32(2.0) * s * s, F32(2.0) * s * c_


def kernel(pair_ref, leg, grid_hbm, pair_v, vert, out,
           grid, even, odd, pairs, table, base_a, base_b, xs, xr, perm, zs, zr,
           wide, mixed, leg1, leg2, rs, rr, own,
           grid_sem, legl_sem, legs_sem, legr_sem, xs_sem, xr_sem, zl_sem, zs_sem, zr_sem, rs_sem, rr_sem):
    lat = lax.axis_index("lat")
    lev = lax.axis_index("lev")
    x, y = lat // 4, lat % 4

    def at_x(d):
        return (lax.rem(x + d, 4) * 4 + y, lev)

    def at_y(d):
        return (x * 4 + lax.rem(y + d, 4), lev)

    def at_z(e):
        return (lat, lax.rem(lev + e, 16))

    barrier = pltpu.get_barrier_semaphore()
    peers = [at_x(d) for d in (1, 2, 3)] + [at_y(d) for d in (1, 2, 3)] + [at_z(e) for e in range(1, 16)]
    for peer in peers:
        pl.semaphore_signal(barrier, inc=1, device_id=peer, device_id_type=MESH)

    grid_copy = pltpu.make_async_copy(grid_hbm, grid, grid_sem)
    grid_copy.start()

    local, remote = [], []
    for d in DIST:
        sy, sx = lax.rem(y + d, 4), lax.rem(x + d, 4)
        local.append((
            pltpu.make_async_copy(leg.at[x, sy, 0], leg1.at[sy, pl.ds(x * 5, 5)], legl_sem.at[0, d]),
            pltpu.make_async_copy(leg.at[sx, y, 1], leg2.at[sx, pl.ds(4 + y * 5, 5)], legl_sem.at[1, d]),
        ))
        group = []
        for e in (1, 3, 2):
            px, py = lax.rem(x + e, 4), lax.rem(y + e, 4)
            group.append(pltpu.make_async_remote_copy(
                src_ref=leg.at[px, sy, 0], dst_ref=leg1.at[sy, pl.ds(x * 5, 5)],
                send_sem=legs_sem.at[0, d, e], recv_sem=legr_sem.at[0, d, e],
                device_id=at_x(e), device_id_type=MESH))
            group.append(pltpu.make_async_remote_copy(
                src_ref=leg.at[sx, py, 1], dst_ref=leg2.at[sx, pl.ds(4 + y * 5, 5)],
                send_sem=legs_sem.at[1, d, e], recv_sem=legr_sem.at[1, d, e],
                device_id=at_y(e), device_id_type=MESH))
        remote.append(group)

    pairs[0:4] = pair_v[...]
    pairs[4:8] = jnp.zeros((4, 128), jnp.int32)

    def columns(g, d):
        t = iota((8, 128), 1)
        s = (t >> 1) & 3
        there = (lev + (4 + 8 * g) + ((t >> 3) & 7)) & 15
        dx, dy = lax.rem(x + d, 4), lax.rem(y + d, 4)
        index = there * 32 + jnp.where(t < 64, dx * 8 + s * 2, s * 8 + dy * 2 + 1)
        got = jnp.take_along_axis(pairs[...], index & 127, axis=1)
        mine = iota((8, 128), 0) == (index >> 7)
        return jnp.sum(jnp.where(mine, got, 0).astype(F32), axis=0, keepdims=True)

    def make_table(buf, g, q):
        for n in range(2):
            d = DIST[2 * q + n]
            p = columns(g, d)
            high = (iota((24, 128), 0) * (2 * LOW)).astype(F32)
            cos, sin = cos_sin(high * p)
            imag = (iota((24, 128), 1) & 1) == 1
            factor = F32(1.0 / math.sqrt(NLON))
            base_a[buf, n] = jnp.where(imag, -sin, cos) * factor
            base_b[buf, n] = jnp.where(imag, -cos, -sin) * factor
            for o in range(2):
                low = (iota((LOW, 128), 0) * 2 + o).astype(F32)
                cos, sin = cos_sin(low * p)
                for i in range(HIGH):
                    block = base_a[buf, n, i:i + 1] * cos + base_b[buf, n, i:i + 1] * sin
                    table[buf, o, i * LOW:(i + 1) * LOW, n * 128:(n + 1) * 128] = block.astype(BF16)

    row, col = iota((256, 256), 0), iota((256, 256), 1)
    parted = (row == 2 * (col & 127) + (col >> 7)).astype(BF16)
    row, col = iota((128, 128), 0), iota((128, 128), 1)
    want = ((row >> 3) & 1) * 64 + (row >> 4) * 8 + (row & 7)
    minus = (((row >> 3) & 1) == 1) & ((row & 1) == 1)
    perm[...] = jnp.where(col == want, jnp.where(minus, F32(-1.0), F32(1.0)), F32(0.0)).astype(BF16)

    make_table(0, 0, 0)
    grid_copy.wait()
    for b in range(NLON // 256):
        halves = jnp.dot(grid[:, :, b * 256:(b + 1) * 256].reshape(320, 256), parted,
                         preferred_element_type=F32).astype(BF16)
        even[:, b * 128:(b + 1) * 128] = halves[:, 0:128]
        odd[:, b * 128:(b + 1) * 128] = halves[:, 128:256]

    pl.semaphore_wait(barrier, len(peers))
    for copy in remote[0][0:4]:
        copy.start()
    for pair in local:
        for copy in pair:
            copy.start()

    lane_low = iota((320, 128), 1) < 64
    x_copies = []
    for g in range(2):
        for q in range(2):
            buf = q
            if g + q > 0:
                make_table(buf, g, q)
            a = jnp.dot(even[...], table[buf, 0], preferred_element_type=F32)
            b = jnp.dot(odd[...], table[buf, 1], preferred_element_type=F32)
            for n in range(2):
                d = DIST[2 * q + n]
                plus = (a + b)[:, n * 128:(n + 1) * 128]
                less = (a - b)[:, n * 128:(n + 1) * 128]
                for h in range(2):
                    if h == 0:
                        part = jnp.where(lane_low, plus, pltpu.roll(less, 64, 1))
                    else:
                        part = jnp.where(lane_low, pltpu.roll(plus, 64, 1), less)
                    part = part.astype(BF16).reshape(4, 80, 128)
                    here = x if h == 0 else 4 + y
                    if d == 0:
                        xr[g, :, here] = part
                        continue
                    xs[g, d - 1, h] = part
                    copy = pltpu.make_async_remote_copy(
                        src_ref=xs.at[g, d - 1, h], dst_ref=xr.at[g, :, here],
                        send_sem=xs_sem.at[g, h, d], recv_sem=xr_sem.at[g, h, d],
                        device_id=at_x(d) if h == 0 else at_y(d), device_id_type=MESH)
                    copy.start()
                    x_copies.append((g, copy))
        if g == 0:
            for copy in remote[0][4:]:
                copy.start()
    for copy in remote[1]:
        copy.start()

    z_copies = []
    for g in range(2):
        for gg, copy in x_copies:
            if gg == g:
                copy.wait()
        for l in range(4):
            turned = lax.dot_general(perm[...], xr[g, l].reshape(640, 128), (((1,), (1,)), ((), ())),
                                     preferred_element_type=F32).astype(BF16)
            zs[g, :, l] = turned.reshape(8, 16, 640)
        for i in ((4, 3, 5, 2, 6, 1, 7, 0), (0, 7, 1, 6, 2, 5, 3))[g]:
            e = (4 + 8 * g + i) % 16
            copy = pltpu.make_async_remote_copy(
                src_ref=zs.at[g, i], dst_ref=zr.at[lev],
                send_sem=zs_sem.at[e], recv_sem=zr_sem.at[e],
                device_id=at_z(e), device_id_type=MESH)
            copy.start()
            z_copies.append(copy)
        for copy in remote[2 + g]:
            copy.start()
    z_own = pltpu.make_async_copy(zs.at[1, 4], zr.at[lev], zl_sem)
    z_own.start()

    leg1[:, 20:24] = jnp.zeros((4, 4, 16, ROWS), BF16)
    leg2[:, 0:4] = jnp.zeros((4, 4, 16, ROWS), BF16)
    level_of = ((iota((64, 1024), 1) >> 4) == iota((64, 1024), 0)).astype(BF16)
    spread = jnp.dot(vert[...], level_of, preferred_element_type=F32)
    inner = iota((64, 1024), 1) & 15
    for s in range(4):
        for u in range(2):
            for c in range(2):
                i = s * 4 + u * 2 + c
                wide[i * 64:(i + 1) * 64, :] = jnp.where(inner == u * 8 + s * 2 + c, spread, F32(0.0)).astype(BF16)

    z_own.wait()
    for copy in z_copies:
        copy.wait()
    mixed[...] = jnp.dot(wide[...], zr[...].reshape(1024, 640), preferred_element_type=F32).astype(BF16)

    def summed(h, d, part):
        s = lax.rem((y if h == 0 else x) + d, 4)
        legs = leg1 if h == 0 else leg2
        lanes = slice(0, 384) if h == 0 else slice(256, 640)
        table_half = legs[s, :, :, part * HALF:(part + 1) * HALF].reshape(384, HALF)
        if part == 0:
            g = mixed[pl.ds(pl.multiple_of(s * 256, 256), 128), lanes]
            return jnp.dot(g, table_half, preferred_element_type=F32)
        slot = lev * 32 + ((x * 4 + s) * 2 if h == 0 else (s * 4 + y) * 2 + 1)
        g = mixed[pl.ds(pl.multiple_of(s * 256, 256), 256), lanes]
        both = jnp.dot(g, table_half, preferred_element_type=F32)
        first = iota((128, HALF), 1) + HALF < NDEG - pair_ref[slot]
        return jnp.where(first, both[0:128], both[128:256])

    def arrived(n):
        for copy in local[n]:
            copy.wait()
        for copy in remote[n]:
            copy.wait()

    out_copies = {}

    def send(h, k, part, value):
        rs[h, k, part] = value.astype(BF16)
        step = (1, 1, 3)[k] if k > 0 else (1, 3)[part]
        copy = pltpu.make_async_remote_copy(
            src_ref=rs.at[h, k, part], dst_ref=rr.at[h, k, part],
            send_sem=rs_sem.at[h, k, part], recv_sem=rr_sem.at[h, k, part],
            device_id=at_y(step) if h == 0 else at_x(step), device_id_type=MESH)
        copy.start()
        out_copies[h, k, part] = copy

    arrived(0)
    for h in range(2):
        for part in range(2):
            send(h, 0, part, summed(h, 2, part))
    arrived(1)
    for h in range(2):
        send(h, 1, 1, summed(h, 1, 1))
    arrived(2)
    for h in range(2):
        send(h, 2, 0, summed(h, 3, 0))
    for k, part in ((1, 0), (2, 1)):
        for h in range(2):
            value = summed(h, 1 if k == 1 else 3, part)
            out_copies[h, 0, part].wait()
            send(h, k, part, value + rr[h, 0, part].astype(F32))
    arrived(3)
    for h in range(2):
        for part in range(2):
            own[h, part] = summed(h, 0, part)
    for part in range(2):
        for h in range(2):
            for k in (1, 2):
                out_copies[h, k, part].wait()
            for r in range(0, HALF, 128):
                total = own[h, part, :, r:r + 128]
                for k in (1, 2):
                    total = total + rr[h, k, part, :, r:r + 128].astype(F32)
                out[0, h, part * HALF + r:part * HALF + r + 128, :] = total.T.astype(BF16)


def body(grid, pair_index, legendre, vertical):
    vmem = pl.BlockSpec(memory_space=pltpu.VMEM)
    hbm = pl.BlockSpec(memory_space=pl.ANY)
    dma = pltpu.SemaphoreType.DMA
    return pl.pallas_call(
        kernel,
        out_shape=jax.ShapeDtypeStruct((1, 2, ROWS, 128), BF16),
        in_specs=[pl.BlockSpec(memory_space=pltpu.SMEM), hbm, hbm, vmem, vmem],
        out_specs=vmem,
        scratch_shapes=[
            pltpu.VMEM((4, 80, NLON), BF16),
            pltpu.VMEM((320, NLON // 2), BF16),
            pltpu.VMEM((320, NLON // 2), BF16),
            pltpu.VMEM((8, 128), jnp.int32),
            pltpu.VMEM((2, 2, NLON // 2, 256), BF16),
            pltpu.VMEM((2, 2, 24, 128), F32),
            pltpu.VMEM((2, 2, 24, 128), F32),
            pltpu.VMEM((2, 3, 2, 4, 80, 128), BF16),
            pltpu.VMEM((2, 4, 8, 80, 128), BF16),
            pltpu.VMEM((128, 128), BF16),
            pltpu.VMEM((2, 8, 4, 16, 640), BF16),
            pltpu.VMEM((16, 4, 16, 640), BF16),
            pltpu.VMEM((1024, 1024), BF16),
            pltpu.VMEM((1024, 640), BF16),
            pltpu.VMEM((4, 24, 16, ROWS), BF16),
            pltpu.VMEM((4, 24, 16, ROWS), BF16),
            pltpu.VMEM((2, 3, 2, 128, HALF), BF16),
            pltpu.VMEM((2, 3, 2, 128, HALF), BF16),
            pltpu.VMEM((2, 2, 128, HALF), F32),
            dma, dma((2, 4)), dma((2, 4, 4)), dma((2, 4, 4)), dma((2, 2, 4)), dma((2, 2, 4)),
            dma, dma((16,)), dma((16,)), dma((2, 3, 2)), dma((2, 3, 2)),
        ],
        compiler_params=pltpu.CompilerParams(
            collective_id=0, has_side_effects=True, vmem_limit_bytes=56 * 1024 * 1024),
        cost_estimate=pl.CostEstimate(flops=8_000_000_000, bytes_accessed=12_000_000, transcendentals=0),
        name="spectral",
    )(pair_index, legendre.reshape(4, 4, 2, 5, 16, ROWS), grid, pair_index.reshape(4, 128), vertical)


def solution(mesh):
    placed = (P("lev", "lat", None), P(), P("lev", "lat", None), P())
    return jax.shard_map(
        body, mesh=mesh, in_specs=placed, out_specs=P("lev", "lat", None, None), check_vma=False
    )
```

time: 347 us -> 73.8 us (0.21)
  the two profiles are of different devices: /device:TPU:28 before, /device:TPU:1 now
where the time goes in v2:
time: 73.8 us; the launch traced here: 73.6 us
  Pallas kernels  71.6 us (97%)
  local copies, waits for them, and re-layouts  1.97 us (3%)
    pallas_call x1, Pallas kernels, body(): pl.pallas_call(kernel, out_shape=jax.ShapeDtypeStruct((1, 2, ROWS, 128),...  71.6 us
    unnamed x1, local copies, waits for them, and re-layouts  1.97 us

profile of v2, /device:TPU:1, one launch (start us, length us, event | category | flops | bytes accessed | tf_op | source)
XLA Modules:
  0.0 73.6 jit_solution(312054255889214560)
XLA Ops:
  0.0 71.6 %spectral.1 = bf16[1,2,1280,128]{3,2,1,0:T(8,128)(2,1)} custom-call(s32[512]{0:T(512)} %pair_ref.1, bf16[4,4,2,5,16,1280]{5,4,3,2,1,0:T(8,128)(2,1)} %bitcast.2, bf16[4,80,2560]{2,1,0:T(8,128)(2,1)} %grid_hbm.1, s32[4,128]{1,0:T(4,128)} %bitcast.3, bf16[64,64]{1,0:T(8,128)(2,1)} %vert.1), custom_call_target="tpu_custom_call" | custom-call | flops 8000000000 | bytes 12000000 | tf_op jit(solution)/shard_map/spectral/pallas_call | solution.py:277
  71.6 2.0 %copy.6 = bf16[1,2,1280,128]{3,2,1,0:T(8,128)(2,1)} copy(bf16[1,2,1280,128]{3,2,1,0:T(8,128)(2,1)} %spectral.1) | data formatting | bytes 1310720

commit v3 on v2

--- a/solution.py
+++ b/solution.py
@@ -17,6 +17,7 @@
 LOW = 64
 HIGH = NLON // 2 // LOW
 DIST = (2, 1, 3, 0)
+VMEM_MIB = 52
 
 
 def iota(shape, dim):
@@ -37,10 +38,10 @@
     return F32(1.0) - F32(2.0) * s * s, F32(2.0) * s * c_
 
 
-def kernel(pair_ref, leg, grid_hbm, pair_v, vert, out,
-           grid, even, odd, pairs, table, base_a, base_b, xs, xr, perm, zs, zr,
-           wide, mixed, leg1, leg2, rs, rr, own,
-           grid_sem, legl_sem, legs_sem, legr_sem, xs_sem, xr_sem, zl_sem, zs_sem, zr_sem, rs_sem, rr_sem):
+def kernel(leg, grid_hbm, pair_hbm, vert_hbm, out,
+           grid, vert, even, odd, pairs, table, base_a, base_b, xs, xr, perm, zs, zr,
+           wide, half_mixed, mixed, leg1, leg2, rs, rr, own,
+           in_sem, legl_sem, legs_sem, legr_sem, xs_sem, xr_sem, zl_sem, zs_sem, zr_sem, rs_sem, rr_sem):
     lat = lax.axis_index("lat")
     lev = lax.axis_index("lev")
     x, y = lat // 4, lat % 4
@@ -59,8 +60,12 @@
     for peer in peers:
         pl.semaphore_signal(barrier, inc=1, device_id=peer, device_id_type=MESH)
 
-    grid_copy = pltpu.make_async_copy(grid_hbm, grid, grid_sem)
+    pair_copy = pltpu.make_async_copy(pair_hbm, pairs.at[pl.ds(0, 4)], in_sem.at[0])
+    grid_copy = pltpu.make_async_copy(grid_hbm, grid, in_sem.at[1])
+    vert_copy = pltpu.make_async_copy(vert_hbm, vert, in_sem.at[2])
+    pair_copy.start()
     grid_copy.start()
+    vert_copy.start()
 
     local, remote = [], []
     for d in DIST:
@@ -82,8 +87,10 @@
                 device_id=at_y(e), device_id_type=MESH))
         remote.append(group)
 
-    pairs[0:4] = pair_v[...]
-    pairs[4:8] = jnp.zeros((4, 128), jnp.int32)
+    pl.semaphore_wait(barrier, len(peers))
+    for copy in remote[0][0:4]:
+        copy.start()
+
 
     def columns(g, d):
         t = iota((8, 128), 1)
@@ -119,6 +126,8 @@
     minus = (((row >> 3) & 1) == 1) & ((row & 1) == 1)
     perm[...] = jnp.where(col == want, jnp.where(minus, F32(-1.0), F32(1.0)), F32(0.0)).astype(BF16)
 
+    pairs[4:8] = jnp.zeros((4, 128), jnp.int32)
+    pair_copy.wait()
     make_table(0, 0, 0)
     grid_copy.wait()
     for b in range(NLON // 256):
@@ -126,13 +135,6 @@
                          preferred_element_type=F32).astype(BF16)
         even[:, b * 128:(b + 1) * 128] = halves[:, 0:128]
         odd[:, b * 128:(b + 1) * 128] = halves[:, 128:256]
-
-    pl.semaphore_wait(barrier, len(peers))
-    for copy in remote[0][0:4]:
-        copy.start()
-    for pair in local:
-        for copy in pair:
-            copy.start()
 
     lane_low = iota((320, 128), 1) < 64
     x_copies = []
@@ -167,6 +169,9 @@
         if g == 0:
             for copy in remote[0][4:]:
                 copy.start()
+            for pair in local:
+                for copy in pair:
+                    copy.start()
     for copy in remote[1]:
         copy.start()
 
@@ -182,19 +187,22 @@
         for i in ((4, 3, 5, 2, 6, 1, 7, 0), (0, 7, 1, 6, 2, 5, 3))[g]:
             e = (4 + 8 * g + i) % 16
             copy = pltpu.make_async_remote_copy(
-                src_ref=zs.at[g, i], dst_ref=zr.at[lev],
+                src_ref=zs.at[g, i], dst_ref=zr.at[g, i],
                 send_sem=zs_sem.at[e], recv_sem=zr_sem.at[e],
                 device_id=at_z(e), device_id_type=MESH)
             copy.start()
-            z_copies.append(copy)
+            z_copies.append((g, copy))
         for copy in remote[2 + g]:
             copy.start()
-    z_own = pltpu.make_async_copy(zs.at[1, 4], zr.at[lev], zl_sem)
+    z_own = pltpu.make_async_copy(zs.at[1, 4], zr.at[1, 4], zl_sem)
     z_own.start()
 
     leg1[:, 20:24] = jnp.zeros((4, 4, 16, ROWS), BF16)
     leg2[:, 0:4] = jnp.zeros((4, 4, 16, ROWS), BF16)
-    level_of = ((iota((64, 1024), 1) >> 4) == iota((64, 1024), 0)).astype(BF16)
+    vert_copy.wait()
+    col = iota((64, 1024), 1)
+    level = ((lev + 12 - (col >> 6)) & 15) * 4 + ((col >> 4) & 3)
+    level_of = (level == iota((64, 1024), 0)).astype(BF16)
     spread = jnp.dot(vert[...], level_of, preferred_element_type=F32)
     inner = iota((64, 1024), 1) & 15
     for s in range(4):
@@ -203,10 +211,16 @@
                 i = s * 4 + u * 2 + c
                 wide[i * 64:(i + 1) * 64, :] = jnp.where(inner == u * 8 + s * 2 + c, spread, F32(0.0)).astype(BF16)
 
+    for g, copy in z_copies:
+        if g == 0:
+            copy.wait()
+    half_mixed[...] = jnp.dot(wide[:, 0:512], zr[0].reshape(512, 640), preferred_element_type=F32)
     z_own.wait()
-    for copy in z_copies:
-        copy.wait()
-    mixed[...] = jnp.dot(wide[...], zr[...].reshape(1024, 640), preferred_element_type=F32).astype(BF16)
+    for g, copy in z_copies:
+        if g == 1:
+            copy.wait()
+    mixed[...] = (half_mixed[...] + jnp.dot(wide[:, 512:1024], zr[1].reshape(512, 640),
+                                            preferred_element_type=F32)).astype(BF16)
 
     def summed(h, d, part):
         s = lax.rem((y if h == 0 else x) + d, 4)
@@ -219,7 +233,9 @@
         slot = lev * 32 + ((x * 4 + s) * 2 if h == 0 else (s * 4 + y) * 2 + 1)
         g = mixed[pl.ds(pl.multiple_of(s * 256, 256), 256), lanes]
         both = jnp.dot(g, table_half, preferred_element_type=F32)
-        first = iota((128, HALF), 1) + HALF < NDEG - pair_ref[slot]
+        mine = iota((8, 128), 0) * 128 + iota((8, 128), 1) == slot
+        p = jnp.sum(jnp.where(mine, pairs[...], 0).astype(F32), keepdims=True).astype(jnp.int32)
+        first = iota((128, HALF), 1) + HALF < NDEG - p
         return jnp.where(first, both[0:128], both[128:256])
 
     def arrived(n):
@@ -277,10 +293,11 @@
     return pl.pallas_call(
         kernel,
         out_shape=jax.ShapeDtypeStruct((1, 2, ROWS, 128), BF16),
-        in_specs=[pl.BlockSpec(memory_space=pltpu.SMEM), hbm, hbm, vmem, vmem],
+        in_specs=[hbm, hbm, hbm, hbm],
         out_specs=vmem,
         scratch_shapes=[
             pltpu.VMEM((4, 80, NLON), BF16),
+            pltpu.VMEM((64, 64), BF16),
             pltpu.VMEM((320, NLON // 2), BF16),
             pltpu.VMEM((320, NLON // 2), BF16),
             pltpu.VMEM((8, 128), jnp.int32),
@@ -291,22 +308,23 @@
             pltpu.VMEM((2, 4, 8, 80, 128), BF16),
             pltpu.VMEM((128, 128), BF16),
             pltpu.VMEM((2, 8, 4, 16, 640), BF16),
-            pltpu.VMEM((16, 4, 16, 640), BF16),
+            pltpu.VMEM((2, 8, 4, 16, 640), BF16),
             pltpu.VMEM((1024, 1024), BF16),
+            pltpu.VMEM((1024, 640), F32),
             pltpu.VMEM((1024, 640), BF16),
             pltpu.VMEM((4, 24, 16, ROWS), BF16),
             pltpu.VMEM((4, 24, 16, ROWS), BF16),
             pltpu.VMEM((2, 3, 2, 128, HALF), BF16),
             pltpu.VMEM((2, 3, 2, 128, HALF), BF16),
             pltpu.VMEM((2, 2, 128, HALF), F32),
-            dma, dma((2, 4)), dma((2, 4, 4)), dma((2, 4, 4)), dma((2, 2, 4)), dma((2, 2, 4)),
+            dma((3,)), dma((2, 4)), dma((2, 4, 4)), dma((2, 4, 4)), dma((2, 2, 4)), dma((2, 2, 4)),
             dma, dma((16,)), dma((16,)), dma((2, 3, 2)), dma((2, 3, 2)),
         ],
         compiler_params=pltpu.CompilerParams(
-            collective_id=0, has_side_effects=True, vmem_limit_bytes=56 * 1024 * 1024),
+            collective_id=0, has_side_effects=True, vmem_limit_bytes=VMEM_MIB * 1024 * 1024),
         cost_estimate=pl.CostEstimate(flops=8_000_000_000, bytes_accessed=12_000_000, transcendentals=0),
         name="spectral",
-    )(pair_index, legendre.reshape(4, 4, 2, 5, 16, ROWS), grid, pair_index.reshape(4, 128), vertical)
+    )(legendre.reshape(4, 4, 2, 5, 16, ROWS), grid, pair_index.reshape(4, 128), vertical)
 
 
 def solution(mesh):

time: 73.8 us -> 71.4 us (0.967)
  Pallas kernels: 71.6 us -> 69 us
    pallas_call x1, Pallas kernels: 71.6 us -> 69 us  [body(): pl.pallas_call(kernel, out_shape=jax.ShapeDtypeStruct((1, 2, ROWS, 128),...]
    unnamed x1 -> x5, local copies, waits for them, and re-layouts: 1.97 us -> 2.24 us
where the time goes in v3:
time: 71.4 us; the launch traced here: 71.2 us
  Pallas kernels  69 us (97%)
  local copies, waits for them, and re-layouts  2.24 us (3%)
    pallas_call x1, Pallas kernels, body(): pl.pallas_call(kernel, out_shape=jax.ShapeDtypeStruct((1, 2, ROWS, 128),...  69 us
    unnamed x5, local copies, waits for them, and re-layouts  2.24 us

profile of v3, /device:TPU:1, one launch (start us, length us, event | category | flops | bytes accessed | tf_op | source)
XLA Modules:
  0.0 71.2 jit_solution(13319886170060818176)
XLA Ops:
  0.0 0.0 copy-start
  0.0 0.7 %copy-done = bf16[64,64]{1,0:T(8,128)(2,1)S(1)} copy-done((bf16[64,64]{1,0:T(8,128)(2,1)S(1)}, bf16[64,64]{1,0:T(8,128)(2,1)}, u32[]{:S(2)}) %copy-start) | copy-done | bytes 8216
  0.7 0.0 copy-start.1
  0.7 0.7 copy-done.1
  1.4 69.0 %spectral.1 = bf16[1,2,1280,128]{3,2,1,0:T(8,128)(2,1)S(1)} custom-call(bf16[4,4,2,5,16,1280]{5,4,3,2,1,0:T(8,128)(2,1)} %bitcast.3, bf16[4,80,2560]{2,1,0:T(8,128)(2,1)} %grid_hbm.1, s32[4,128]{1,0:T(4,128)S(1)} %bitcast.2, bf16[64,64]{1,0:T(8,128)(2,1)S(1)} %copy-done), custom_call_target="tpu_custom_call" | custom-call | flops 8000000000 | bytes 12000000 | tf_op jit(solution)/shard_map/spectral/pallas_call | solution.py:293
  70.4 0.8 %copy.6 = bf16[1,2,1280,128]{3,2,1,0:T(8,128)(2,1)} copy(bf16[1,2,1280,128]{3,2,1,0:T(8,128)(2,1)S(1)} %spectral.1) | data formatting | bytes 1310720
Async XLA Ops:
  0.0 0.7 %copy-start = (bf16[64,64]{1,0:T(8,128)(2,1)S(1)}, bf16[64,64]{1,0:T(8,128)(2,1)}, u32[]{:S(2)}) copy-start(bf16[64,64]{1,0:T(8,128)(2,1)} %vert_hbm.1) | copy-start | bytes 24580
  0.7 0.7 copy-start.1

commit v4 on v3

v4 whole, which is shorter than its diff:
```python
import math

import jax
import jax.numpy as jnp
from jax import lax
from jax.sharding import PartitionSpec as P
from jax.experimental import pallas as pl
from jax.experimental.pallas import tpu as pltpu

MESH = pl.DeviceIdType.MESH
F32 = jnp.float32
BF16 = jnp.bfloat16
NLON = 2560
NDEG = 1280
ROWS = 1280
HALF = ROWS // 2
LOW = 64
HIGH = NLON // 2 // LOW
BLOCKS = ((1, 2), (2, 3), (0, 1), (3, 0))
CHUNKS = (((0, 2), (0, 3), (0, 4), (0, 5)), ((0, 0), (0, 1), (0, 6), (0, 7)),
          ((1, 0), (1, 1), (1, 6), (1, 7)), ((1, 2), (1, 3), (1, 4), (1, 5)))
VMEM_MIB = 52


def iota(shape, dim):
    return lax.broadcasted_iota(jnp.int32, shape, dim)


def cos_sin(number):
    whole = jnp.floor(number * F32(1.0 / NLON) + F32(0.5))
    h = (number - whole * F32(NLON)) * F32(math.pi / NLON)
    h2 = h * h
    s = F32(-1.0 / 39916800.0)
    for c in (1.0 / 362880.0, -1.0 / 5040.0, 1.0 / 120.0, -1.0 / 6.0, 1.0):
        s = s * h2 + F32(c)
    s = s * h
    c_ = F32(1.0 / 479001600.0)
    for c in (-1.0 / 3628800.0, 1.0 / 40320.0, -1.0 / 720.0, 1.0 / 24.0, -0.5, 1.0):
        c_ = c_ * h2 + F32(c)
    return F32(1.0) - F32(2.0) * s * s, F32(2.0) * s * c_


def kernel(leg, grid_hbm, pair_hbm, vert_hbm, out,
           grid, vert, even, odd, pairs, limit, table, base_a, base_b, xs, xr, perm, spread, zs, zr,
           mixed, legs, t1, r1, rs, rr, keep, own, total, wide,
           in_sem, legl_sem, legs_sem, legr_sem, xs_sem, xr_sem, zs_sem, zr_sem,
           ts_sem, tr_sem, rs_sem, rr_sem):
    lat = lax.axis_index("lat")
    lev = lax.axis_index("lev")
    x, y = lat // 4, lat % 4

    def at(axis, d):
        if axis == 0:
            return (lax.rem(x + d, 4) * 4 + y, lev)
        return (x * 4 + lax.rem(y + d, 4), lev)

    def at_z(e):
        return (lat, lax.rem(lev + e, 16))

    barrier = pltpu.get_barrier_semaphore()
    peers = [at(axis, d) for axis in (0, 1) for d in (1, 3)] + [at_z(e) for e in range(1, 16)]
    for peer in peers:
        pl.semaphore_signal(barrier, inc=1, device_id=peer, device_id_type=MESH)

    pair_copy = pltpu.make_async_copy(pair_hbm, pairs.at[pl.ds(0, 4)], in_sem.at[0])
    grid_copy = pltpu.make_async_copy(grid_hbm, grid, in_sem.at[1])
    vert_copy = pltpu.make_async_copy(vert_hbm, vert, in_sem.at[2])
    pair_copy.start()
    grid_copy.start()
    vert_copy.start()

    def source(h, d, s):
        if h == 0:
            return leg.at[lax.rem(x + d, 4), s, 0]
        return leg.at[s, lax.rem(y + d, 4), 1]

    local, remote = [], []
    for s in range(4):
        for h in range(2):
            for n in range(2):
                to = BLOCKS[n][s % 2]
                first = (2 * h + n) * 2
                remote.append(pltpu.make_async_remote_copy(
                    src_ref=source(h, to, s), dst_ref=legs.at[h, n, s, pl.ds(first + 5 * n, 5)],
                    send_sem=legs_sem.at[h, n, s], recv_sem=legr_sem.at[h, n, s],
                    device_id=at(h, 1 if n == 0 else 3), device_id_type=MESH))
                to = BLOCKS[2 + n][s % 2]
                local.append(pltpu.make_async_copy(
                    source(h, to, s), legs.at[h, n, s, pl.ds(first + 5 - 5 * n, 5)], legl_sem.at[h, n, s]))

    pl.semaphore_wait(barrier, len(peers))
    for copy in remote[0:4]:
        copy.start()

    def columns(g, n):
        t = iota((8, 128), 1)
        s = (t >> 1) & 3
        there = (lev + (12 + 8 * g) + ((t >> 3) & 7)) & 15
        ahead = jnp.where((s & 1) == 1, BLOCKS[n][1], BLOCKS[n][0])
        index = there * 32 + jnp.where(t < 64, ((x + ahead) & 3) * 8 + s * 2, s * 8 + ((y + ahead) & 3) * 2 + 1)
        got = jnp.take_along_axis(pairs[...], index & 127, axis=1)
        mine = iota((8, 128), 0) == (index >> 7)
        return jnp.sum(jnp.where(mine, got, 0).astype(F32), axis=0, keepdims=True)

    def make_table(buf, g, q):
        for n in range(2):
            p = columns(g, 2 * q + n)
            high = (iota((24, 128), 0) * (2 * LOW)).astype(F32)
            cos, sin = cos_sin(high * p)
            imag = (iota((24, 128), 1) & 1) == 1
            factor = F32(1.0 / math.sqrt(NLON))
            base_a[buf, n] = jnp.where(imag, -sin, cos) * factor
            base_b[buf, n] = jnp.where(imag, -cos, -sin) * factor
            for o in range(2):
                low = (iota((LOW, 128), 0) * 2 + o).astype(F32)
                cos, sin = cos_sin(low * p)
                for i in range(HIGH):
                    block = base_a[buf, n, i:i + 1] * cos + base_b[buf, n, i:i + 1] * sin
                    table[buf, o, i * LOW:(i + 1) * LOW, n * 128:(n + 1) * 128] = block.astype(BF16)

    row, col = iota((256, 256), 0), iota((256, 256), 1)
    parted = (row == 2 * (col & 127) + (col >> 7)).astype(BF16)
    row, col = iota((128, 128), 0), iota((128, 128), 1)
    want = ((row >> 3) & 1) * 64 + (row >> 4) * 8 + (row & 7)
    minus = (((row >> 3) & 1) == 1) & ((row & 1) == 1)
    perm[...] = jnp.where(col == want, jnp.where(minus, F32(-1.0), F32(1.0)), F32(0.0)).astype(BF16)

    pairs[4:8] = jnp.zeros((4, 128), jnp.int32)
    pair_copy.wait()
    make_table(0, 0, 0)
    grid_copy.wait()
    for b in range(NLON // 256):
        halves = jnp.dot(grid[:, :, b * 256:(b + 1) * 256].reshape(320, 256), parted,
                         preferred_element_type=F32).astype(BF16)
        even[:, b * 128:(b + 1) * 128] = halves[:, 0:128]
        odd[:, b * 128:(b + 1) * 128] = halves[:, 128:256]

    lane_low = iota((320, 128), 1) < 64
    x_copies = []
    for g in range(2):
        for q in range(2):
            if g + q > 0:
                make_table(q, g, q)
            a = jnp.dot(even[...], table[q, 0], preferred_element_type=F32)
            b = jnp.dot(odd[...], table[q, 1], preferred_element_type=F32)
            for n in range(2):
                plus = (a + b)[:, n * 128:(n + 1) * 128]
                less = (a - b)[:, n * 128:(n + 1) * 128]
                for h in range(2):
                    if h == 0:
                        part = jnp.where(lane_low, plus, pltpu.roll(less, 64, 1))
                    else:
                        part = jnp.where(lane_low, pltpu.roll(plus, 64, 1), less)
                    part = part.astype(BF16).reshape(4, 80, 128)
                    if q == 1:
                        xr[g, :, h * 4 + 1 + n] = part
                        continue
                    xs[g, n, h] = part
                    copy = pltpu.make_async_remote_copy(
                        src_ref=xs.at[g, n, h], dst_ref=xr.at[g, :, h * 4 + 3 * n],
                        send_sem=xs_sem.at[g, n, h], recv_sem=xr_sem.at[g, n, h],
                        device_id=at(h, 1 if n == 0 else 3), device_id_type=MESH)
                    copy.start()
                    x_copies.append((g, copy))
        for copy in remote[4:8] if g == 0 else remote[8:16]:
            copy.start()
        if g == 0:
            for copy in local:
                copy.start()

    z_copies = {}
    for g in range(2):
        for gg, copy in x_copies:
            if gg == g:
                copy.wait()
        for l in range(4):
            turned = lax.dot_general(perm[...], xr[g, l].reshape(640, 128), (((1,), (1,)), ((), ())),
                                     preferred_element_type=F32).astype(BF16)
            zs[g, :, l] = turned.reshape(8, 16, 640)
            if g == 0:
                zr[0, 2, l] = turned[64:80]
        for q in (2 * g, 2 * g + 1):
            for k, (_, i) in enumerate(CHUNKS[q]):
                e = (12 + 8 * g + i) % 16
                if e == 0:
                    continue
                copy = pltpu.make_async_remote_copy(
                    src_ref=zs.at[g, i], dst_ref=zr.at[q, k],
                    send_sem=zs_sem.at[q, k], recv_sem=zr_sem.at[q, k],
                    device_id=at_z(e), device_id_type=MESH)
                copy.start()
                z_copies[q, k] = copy

    for h in range(2):
        for n in range(2):
            first = (2 * h + n) * 2
            if first > 0:
                legs[h, n, :, 0:first] = jnp.zeros((4, first, 16, ROWS), BF16)
            if first < 6:
                legs[h, n, :, first + 10:16] = jnp.zeros((4, 6 - first, 16, ROWS), BF16)
    row, col = iota((256, 256), 0), iota((256, 256), 1)
    want = (row & 15) * 16 + ((row >> 5) & 1) * 8 + (row >> 6) * 2 + ((row >> 4) & 1)
    spread[...] = (col == want).astype(BF16)
    for h in range(2):
        for role in range(2):
            for s in range(4):
                d = 0 if role == 1 else (1 if s % 2 == 1 else 3)
                if h == 0:
                    slot = lev * 32 + lax.rem(x + d, 4) * 8 + s * 2
                else:
                    slot = lev * 32 + s * 8 + lax.rem(y + d, 4) * 2 + 1
                mine = iota((8, 128), 0) * 128 + iota((8, 128), 1) == slot
                p = jnp.sum(jnp.where(mine, pairs[...], 0).astype(F32), keepdims=True).astype(jnp.int32)
                limit[h, role, s] = NDEG - jnp.broadcast_to(p, (1, ROWS))
    vert_copy.wait()
    row = iota((128, 64), 0)
    q, k = row >> 5, (row >> 2) & 3
    e = jnp.where(q == 0, 14, jnp.where(q == 1, 12, jnp.where(q == 2, 4, 6))) + k
    e = e + jnp.where(((q == 1) | (q == 2)) & (k >= 2), 4, 0)
    level = ((lev + 32 - e) & 15) * 4 + (row & 3)
    chosen = (level == iota((128, 64), 1)).astype(BF16)
    both = jnp.concatenate([vert[...], vert[...]], axis=0)
    twice = lax.dot_general(chosen, both, (((1,), (1,)), ((), ())), preferred_element_type=F32)
    same = ((iota((128, 128), 0) >> 4) & 1) == (iota((128, 128), 1) >> 6)
    wide[...] = jnp.where(same, twice, F32(0.0)).astype(BF16)

    def summed(q, h, n, s, role):
        g = mixed[q, pl.ds(pl.multiple_of(s * 64, 64), 64), pl.ds(pl.multiple_of((2 * h + n) * 128, 128), 256)]
        both = jnp.dot(g, legs[h, n, s].reshape(256, ROWS), preferred_element_type=F32)
        return jnp.where(iota((32, ROWS), 1) < limit[h, role, s], both[0:32], both[32:64])

    out_copies = {}

    def arrive(q):
        for k in range(4):
            if (q, k) in z_copies:
                z_copies[q, k].wait_recv()
                z_copies[q, k].wait_send()
        mixed[q] = jnp.dot(spread[...], zr[q].reshape(256, 640), preferred_element_type=F32).astype(BF16)

    def step_copy(q, h, s):
        return pltpu.make_async_remote_copy(
            src_ref=t1.at[q, h, s], dst_ref=r1.at[q, h, s],
            send_sem=ts_sem.at[q, h, s], recv_sem=tr_sem.at[q, h, s],
            device_id=at(h, 3 - 2 * (s & 1)), device_id_type=MESH)

    def step_on(q, h, s):
        t1[q, h, s] = summed(q, h, 1 - (s & 1), s, 0).astype(BF16)
        step_copy(q, h, s).start()

    def place(h, d):
        return lax.rem((y if h == 0 else x) + d, 4)

    def step_all(q):
        for d in (2, 1, 3, 0):
            for h in range(2):
                step_on(q, h, place(h, d))

    def send(q, h, k, part, value):
        rs[q, h, k, part] = value.astype(BF16)
        step = (1, 1, 3)[k] if k > 0 else (1, 3)[part]
        copy = pltpu.make_async_remote_copy(
            src_ref=rs.at[q, h, k, part], dst_ref=rr.at[q, h, k, part],
            send_sem=rs_sem.at[q, h, k, part], recv_sem=rr_sem.at[q, h, k, part],
            device_id=at(1 - h, step), device_id_type=MESH)
        copy.start()
        out_copies[q, h, k, part] = copy

    def line(q):
        for d in (2, 1, 3, 0):
            for h in range(2):
                s = place(h, d)
                step_copy(q, h, s).wait_recv()
                value = summed(q, h, s & 1, s, 1) + r1[q, h, s].astype(F32)
                if d == 2:
                    send(q, h, 0, 0, value[:, 0:HALF])
                    send(q, h, 0, 1, value[:, HALF:ROWS])
                elif d == 1:
                    send(q, h, 1, 1, value[:, HALF:ROWS])
                    keep[q, h, 0] = value[:, 0:HALF]
                elif d == 3:
                    send(q, h, 2, 0, value[:, 0:HALF])
                    keep[q, h, 1] = value[:, HALF:ROWS]
                else:
                    own[q, h] = value

    def merge(q):
        for part in range(2):
            for h in range(2):
                out_copies[q, h, 0, part].wait()
                send(q, h, 1 + part, part, keep[q, h, part] + rr[q, h, 0, part].astype(F32))

    def finish(q):
        for h in range(2):
            for part in range(2):
                lanes = slice(part * HALF, (part + 1) * HALF)
                value = own[q, h, :, lanes]
                for k in (1, 2):
                    out_copies[q, h, k, part].wait()
                    value = value + rr[q, h, k, part].astype(F32)
                total[h, q * 32:(q + 1) * 32, lanes] = value.astype(BF16)

    arrive(0)
    arrive(1)
    for s in range(4):
        for copy in local[4 * s:4 * s + 4] + remote[4 * s:4 * s + 4]:
            copy.wait()
        for q in range(2):
            for h in range(2):
                step_on(q, h, s)
    line(0)
    line(1)
    merge(0)
    merge(1)
    arrive(2)
    step_all(2)
    arrive(3)
    step_all(3)
    finish(0)
    finish(1)
    line(2)
    line(3)
    merge(2)
    merge(3)
    finish(2)
    finish(3)
    for q in range(4):
        for h in range(2):
            for s in range(4):
                step_copy(q, h, s).wait_send()
    for h in range(2):
        for r in range(0, ROWS, 256):
            coef = total[h, :, r:r + 256].astype(F32).T.astype(BF16)
            out[0, h, r:r + 256, :] = jnp.dot(coef, wide[...], preferred_element_type=F32).astype(BF16)


def body(grid, pair_index, legendre, vertical):
    vmem = pl.BlockSpec(memory_space=pltpu.VMEM)
    hbm = pl.BlockSpec(memory_space=pl.ANY)
    dma = pltpu.SemaphoreType.DMA
    return pl.pallas_call(
        kernel,
        out_shape=jax.ShapeDtypeStruct((1, 2, ROWS, 128), BF16),
        in_specs=[hbm, hbm, hbm, hbm],
        out_specs=vmem,
        scratch_shapes=[
            pltpu.VMEM((4, 80, NLON), BF16),
            pltpu.VMEM((64, 64), BF16),
            pltpu.VMEM((320, NLON // 2), BF16),
            pltpu.VMEM((320, NLON // 2), BF16),
            pltpu.VMEM((8, 128), jnp.int32),
            pltpu.VMEM((2, 2, 4, 1, ROWS), jnp.int32),
            pltpu.VMEM((2, 2, NLON // 2, 256), BF16),
            pltpu.VMEM((2, 2, 24, 128), F32),
            pltpu.VMEM((2, 2, 24, 128), F32),
            pltpu.VMEM((2, 2, 2, 4, 80, 128), BF16),
            pltpu.VMEM((2, 4, 8, 80, 128), BF16),
            pltpu.VMEM((128, 128), BF16),
            pltpu.VMEM((256, 256), BF16),
            pltpu.VMEM((2, 8, 4, 16, 640), BF16),
            pltpu.VMEM((4, 4, 4, 16, 640), BF16),
            pltpu.VMEM((4, 256, 640), BF16),
            pltpu.VMEM((2, 2, 4, 16, 16, ROWS), BF16),
            pltpu.VMEM((4, 2, 4, 32, ROWS), BF16),
            pltpu.VMEM((4, 2, 4, 32, ROWS), BF16),
            pltpu.VMEM((4, 2, 3, 2, 32, HALF), BF16),
            pltpu.VMEM((4, 2, 3, 2, 32, HALF), BF16),
            pltpu.VMEM((4, 2, 2, 32, HALF), F32),
            pltpu.VMEM((4, 2, 32, ROWS), F32),
            pltpu.VMEM((2, 128, ROWS), BF16),
            pltpu.VMEM((128, 128), BF16),
            dma((3,)), dma((2, 2, 4)), dma((2, 2, 4)), dma((2, 2, 4)), dma((2, 2, 2)), dma((2, 2, 2)),
            dma((4, 4)), dma((4, 4)), dma((4, 2, 4)), dma((4, 2, 4)), dma((4, 2, 3, 2)), dma((4, 2, 3, 2)),
        ],
        compiler_params=pltpu.CompilerParams(
            collective_id=0, has_side_effects=True, vmem_limit_bytes=VMEM_MIB * 1024 * 1024),
        cost_estimate=pl.CostEstimate(flops=8_000_000_000, bytes_accessed=12_000_000, transcendentals=0),
        name="spectral",
    )(legendre.reshape(4, 4, 2, 5, 16, ROWS), grid, pair_index.reshape(4, 128), vertical)


def solution(mesh):
    placed = (P("lev", "lat", None), P(), P("lev", "lat", None), P())
    return jax.shard_map(
        body, mesh=mesh, in_specs=placed, out_specs=P("lev", "lat", None, None), check_vma=False
    )
```

time: 71.4 us -> 67.8 us (0.950)
  Pallas kernels: 69 us -> 65.4 us
    pallas_call x1, Pallas kernels: 69 us -> 65.4 us  [body(): pl.pallas_call(kernel, out_shape=jax.ShapeDtypeStruct((1, 2, ROWS, 128),...]
where the time goes in v4:
time: 67.8 us; the launch traced here: 67.7 us
  Pallas kernels  65.4 us (96%)
  local copies, waits for them, and re-layouts  2.24 us (3%)
    pallas_call x1, Pallas kernels, body(): pl.pallas_call(kernel, out_shape=jax.ShapeDtypeStruct((1, 2, ROWS, 128),...  65.4 us
    unnamed x5, local copies, waits for them, and re-layouts  2.24 us

profile of v4, /device:TPU:1, one launch (start us, length us, event | category | flops | bytes accessed | tf_op | source)
XLA Modules:
  0.0 67.7 jit_solution(3477474628432086128)
XLA Ops:
  0.0 0.0 copy-start
  0.0 0.7 %copy-done = bf16[64,64]{1,0:T(8,128)(2,1)S(1)} copy-done((bf16[64,64]{1,0:T(8,128)(2,1)S(1)}, bf16[64,64]{1,0:T(8,128)(2,1)}, u32[]{:S(2)}) %copy-start) | copy-done | bytes 8216
  0.7 0.0 copy-start.1
  0.7 0.7 %copy-done.1 = s32[512]{0:T(512)S(1)} copy-done((s32[512]{0:T(512)S(1)}, s32[512]{0:T(512)}, u32[]{:S(2)}) %copy-start.1) | copy-done | bytes 2072
  1.4 65.4 %spectral.1 = bf16[1,2,1280,128]{3,2,1,0:T(8,128)(2,1)S(1)} custom-call(bf16[4,4,2,5,16,1280]{5,4,3,2,1,0:T(8,128)(2,1)} %bitcast.3, bf16[4,80,2560]{2,1,0:T(8,128)(2,1)} %grid_hbm.1, s32[4,128]{1,0:T(4,128)S(1)} %bitcast.2, bf16[64,64]{1,0:T(8,128)(2,1)S(1)} %copy-done), custom_call_target="tpu_custom_call" | custom-call | flops 8000000000 | bytes 12000000 | tf_op jit(solution)/shard_map/spectral/pallas_call | solution.py:341
  66.8 0.8 %copy.6 = bf16[1,2,1280,128]{3,2,1,0:T(8,128)(2,1)} copy(bf16[1,2,1280,128]{3,2,1,0:T(8,128)(2,1)S(1)} %spectral.1) | data formatting | bytes 1310720
Async XLA Ops:
  0.0 0.7 %copy-start = (bf16[64,64]{1,0:T(8,128)(2,1)S(1)}, bf16[64,64]{1,0:T(8,128)(2,1)}, u32[]{:S(2)}) copy-start(bf16[64,64]{1,0:T(8,128)(2,1)} %vert_hbm.1) | copy-start | bytes 24580
  0.7 0.7 %copy-start.1 = (s32[512]{0:T(512)S(1)}, s32[512]{0:T(512)}, u32[]{:S(2)}) copy-start(s32[512]{0:T(512)} %param.5) | copy-start | bytes 6148
